TPU v7x, 512 devices: a whole 4x4x16 slice. The times are simulated.
512 devices in a mesh: dp: 128 (over z, y, core), grp: 4 (over x).
Axes of the slice: x: 4, y: 4, z: 16, core: 2. Of those that a mesh axis runs over, the one named last changes fastest.
Arguments:
- embeddings: bfloat16 [131072, 1024], P(('dp', 'grp')), may hold values from -24 to 24
- coarse_ids: int32 [131072, 1], P(('dp', 'grp')), may hold values from 0 to 255; in each aligned block of 256 rows (0 to 255, 256 to 511, ...) at most 2 rows name the same one
- owner_slot: int32 [256], replicated, may hold values from 0 to 255, each once
- coarse_centroids: bfloat16 [256, 1024], replicated, may hold values from -6 to 7
- child_centroids: bfloat16 [256, 400, 1024], P('dp'), may hold values from -6 to 7
Outputs:
- new_coarse: float32 [256, 1024], replicated
- new_children: float32 [256, 400, 1024], P('dp', 'grp')
Inputs may be any that keep to these rules, and one draw needn't show every extreme that they name: `coarse_ids`: within the rows of one device no coarse cluster appears more than 2 times, and some cluster appears exactly 2 times in every draw. `owner_slot`: a permutation; the children of coarse cluster c are child_centroids[owner_slot[c]].
All inputs are finite; a program needn't handle non-finite values.
Results may differ from a plain program's by a relative error of at most 0.0004.
Values may be sent and summed in bfloat16 or wider, within the bound.
A program may use at most 64 MiB of HBM per device.

v0:
```python
import jax
import jax.numpy as jnp
from jax import lax
from jax.sharding import PartitionSpec as P

prior_weight = 1.0


def soft_weights(scores):
    highest = jnp.max(scores, axis=-1, keepdims=True)
    raised = jnp.exp(scores - highest)
    return (raised / jnp.sum(raised, axis=-1, keepdims=True)).astype(jnp.bfloat16)


def on_device(embeddings, coarse_ids, owner_slot, coarse_centroids, child_centroids):
    row_count, width = embeddings.shape
    ncoarse = coarse_centroids.shape[0]
    nchild = child_centroids.shape[1]
    capacity = max(2, row_count // 128)
    scale = width ** (-0.5)
    coarse_norms = jnp.einsum(
        "kd,kd->k", coarse_centroids, coarse_centroids, preferred_element_type=jnp.float32
    )
    coarse_products = jnp.einsum(
        "nd,kd->nk", embeddings, coarse_centroids, preferred_element_type=jnp.float32
    )
    coarse_weights = soft_weights((coarse_products - 0.5 * coarse_norms[None, :]) * scale)
    coarse_sums = jnp.einsum(
        "nk,nd->kd", coarse_weights, embeddings, preferred_element_type=jnp.float32
    )
    coarse_mass = jnp.sum(coarse_weights.astype(jnp.float32), axis=0)
    total_sums, total_mass = lax.psum((coarse_sums, coarse_mass), ("dp", "grp"))
    new_coarse = (total_sums + prior_weight * coarse_centroids.astype(jnp.float32)) / (
        total_mass + prior_weight
    )[:, None]
    cluster_iota = lax.broadcasted_iota(jnp.int32, (row_count, ncoarse), 1)
    placed = jnp.sum(jnp.where(coarse_ids == cluster_iota, owner_slot[None, :], 0), axis=1)
    member = (placed[:, None] == cluster_iota).astype(jnp.int32)
    position = jnp.sum((jnp.cumsum(member, axis=0) - member) * member, axis=1)
    target = placed * capacity + position
    outgoing = jnp.zeros((ncoarse * capacity, width), jnp.bfloat16).at[target].set(embeddings)
    outgoing = outgoing.reshape(ncoarse, capacity, width)
    present_out = jnp.zeros((ncoarse * capacity,), jnp.bfloat16).at[target].set(1.0)
    present_out = present_out.reshape(ncoarse, capacity)
    arrived, present = (
        lax.all_to_all(outgoing, "dp", split_axis=0, concat_axis=1, tiled=True),
        lax.all_to_all(present_out, "dp", split_axis=0, concat_axis=1, tiled=True),
    )
    share = nchild // lax.axis_size("grp")
    first_child = lax.axis_index("grp") * share
    child_norms = jnp.einsum(
        "cjd,cjd->cj", child_centroids, child_centroids, preferred_element_type=jnp.float32
    )
    products = jnp.einsum(
        "cnd,cjd->cnj", arrived, child_centroids, preferred_element_type=jnp.float32
    )
    weights = soft_weights((products - 0.5 * child_norms[:, None, :]) * scale) * present[:, :, None]
    child_sums = jnp.einsum("cnj,cnd->cjd", weights, arrived, preferred_element_type=jnp.float32)
    child_mass = jnp.sum(weights.astype(jnp.float32), axis=1)
    mine_sums, mine_mass = (
        lax.psum_scatter(child_sums, "grp", scatter_dimension=1, tiled=True),
        lax.psum_scatter(child_mass, "grp", scatter_dimension=1, tiled=True),
    )
    mine_centers = lax.dynamic_slice_in_dim(child_centroids, first_child, share, 1).astype(
        jnp.float32
    )
    new_children = (mine_sums + prior_weight * mine_centers) / (mine_mass + prior_weight)[
        :, :, None
    ]
    return (new_coarse, new_children)


def solution(mesh):
    return jax.shard_map(
        on_device,
        mesh=mesh,
        in_specs=(P(("dp", "grp"), None), P(("dp", "grp"), None), P(), P(), P("dp", None, None)),
        out_specs=(P(), P("dp", "grp", None)),
        check_vma=False,
    )
```

profile of v0, /device:TPU:1, one launch (start us, length us, event | category | flops | bytes accessed | tf_op | source)
XLA Modules:
  0.0 636.8 jit_solution(2288434667986519832)
XLA Ops:
  7.2 0.9 select_reduce_fusion
  8.0 0.1 copy.13
  8.2 0.2 fusion.12
  8.4 0.0 copy-start
  8.5 0.2 fusion.14
  8.7 2.2 scatter_custom_fusion.1
  10.9 0.8 all_to_all.29
  11.7 20.6 %all-to-all-start.1 = ((bf16[128,2,2]{2,1,0:T(2,128)(2,1)}), bf16[128,2,2]{2,1,0:T(2,128)(2,1)S(1)}, u32[]{:S(2)}, u32[]{:S(2)}) async-start(bf16[128,2,2]{2,1,0:T(2,128)(2,1)} %all_to_all.29), calls=%async_computation.1 | async-start | bytes 131072 | tf_op jit(solution)/shard_map/all_to_all | solution.py:47
  32.3 2.4 scatter_custom_fusion
  34.7 1.2 reshape.66
  35.9 0.0 copy-start.1
  35.9 11.2 %all-to-all-done.1 = bf16[128,2,2]{2,1,0:T(2,128)(2,1)S(1)} async-done(((bf16[128,2,2]{2,1,0:T(2,128)(2,1)}), bf16[128,2,2]{2,1,0:T(2,128)(2,1)S(1)}, u32[]{:S(2)}, u32[]{:S(2)}) %all-to-all-start.1) | async-done | bytes 1056 | tf_op jit(solution)/shard_map/all_to_all | solution.py:47
  47.1 5.7 all-to-all-start
  52.8 0.0 all-reduce.5.cloned.1.call-start
  52.8 0.0 copy-done
  52.8 0.2 fusion.6
  53.0 1.4 fusion.21
  54.4 0.1 fusion.16
  54.5 0.1 convert_reduce_fusion.1
  54.6 2.3 fusion.23
  57.0 0.0 all-reduce.5.cloned.1.call-update
  57.0 0.2 all-reduce.7.cloned.1.call-start
  57.2 0.0 copy-done.1
  57.2 0.4 fusion.1
  57.6 0.1 mul.67
  57.8 47.6 %all-to-all-done = bf16[256,2,1024]{2,1,0:T(2,128)(2,1)S(1)} async-done(((bf16[256,2,1024]{2,1,0:T(2,128)(2,1)}), bf16[256,2,1024]{2,1,0:T(2,128)(2,1)S(1)}, u32[]{:S(2)}, u32[]{:S(2)}) %all-to-all-start) | async-done | bytes 1048608 | tf_op jit(solution)/shard_map/all_to_all | solution.py:46
  105.4 0.7 copy.15
  106.2 0.4 all_to_all.28
  106.6 2.2 fusion.22
  108.8 0.2 convert_reduce_fusion
  109.1 0.6 fusion.24
  109.7 4.2 copy.17
  113.9 0.0 all-reduce.7.cloned.1.call-update
  113.9 1.3 dynamic-slice
  115.9 105.4 %psum.15 = f32[256]{0:T(256)S(1)} all-reduce(f32[256]{0:T(256)S(1)} %get-tuple-element.8), channel_id=1, replica_groups=mesh['dp'=128,'grp'=4] {'dp','grp'}, use_global_device_ids=true, to_apply=%region_4.0 | all-reduce | flops 256 | bytes 2048 | tf_op jit(solution)/shard_map/psum | solution.py:32
  221.2 1.1 constant_dynamic-slice_fusion
  222.4 311.9 %all-reduce.5.cloned.1.call-done = f32[256,1024]{1,0:T(8,128)} async-done(((f32[256,1024]{1,0:T(8,128)}), f32[256,1024]{1,0:T(8,128)}) %all-reduce.5.cloned.1.call-update) | async-done | bytes 1048592 | tf_op jit(solution)/shard_map/psum | solution.py:32
  534.2 2.4 fusion.7
  536.6 8.2 %all-reduce.1 = f32[2,400]{1,0:T(2,128)S(1)} all-reduce(f32[2,400]{1,0:T(2,128)S(1)} %get-tuple-element.6), channel_id=3, replica_groups=mesh['dp'=128,'grp'=4] {'grp'}, use_global_device_ids=true, to_apply=%region_15.16.clone | all-reduce | flops 800 | bytes 6400
  544.9 0.1 dynamic-slice_add_fusion.1
  544.9 0.1 copy.19
  545.1 82.2 %all-reduce.7.cloned.1.call-done = f32[2,400,1024]{2,0,1:T(2,128)} async-done(((f32[2,400,1024]{2,0,1:T(2,128)}), f32[2,400,1024]{2,0,1:T(2,128)}) %all-reduce.7.cloned.1.call-update) | async-done | bytes 3276816
  627.3 2.7 fusion.8
  (13 shorter events, 0.1 us)
Async XLA Ops:
  8.4 44.4 %copy-start = (bf16[256,1024]{1,0:T(8,128)(2,1)S(1)}, bf16[256,1024]{1,0:T(8,128)(2,1)}, u32[]{:S(2)}) copy-start(bf16[256,1024]{1,0:T(8,128)(2,1)} %param.8) | copy-start | bytes 1572868
  11.7 35.4 %all-to-all-start.1 = ((bf16[128,2,2]{2,1,0:T(2,128)(2,1)}), bf16[128,2,2]{2,1,0:T(2,128)(2,1)S(1)}, u32[]{:S(2)}, u32[]{:S(2)}) async-start(bf16[128,2,2]{2,1,0:T(2,128)(2,1)} %all_to_all.29), calls=%async_computation.1 | async-start | bytes 131072 | tf_op jit(solution)/shard_map/all_to_all | solution.py:47
  35.9 21.3 %copy-start.1 = (bf16[2,400,1024]{2,1,0:T(8,128)(2,1)S(1)}, bf16[2,400,1024]{2,1,0:T(8,128)(2,1)}, u32[]{:S(2)}) copy-start(bf16[2,400,1024]{2,1,0:T(8,128)(2,1)} %param.9) | copy-start | bytes 4915204
  47.1 58.3 %all-to-all-start = ((bf16[256,2,1024]{2,1,0:T(2,128)(2,1)}), bf16[256,2,1024]{2,1,0:T(2,128)(2,1)S(1)}, u32[]{:S(2)}, u32[]{:S(2)}) async-start(bf16[256,2,1024]{2,1,0:T(2,128)(2,1)} %reshape.66), calls=%async_computation | async-start | bytes 2097152 | tf_op jit(solution)/shard_map/all_to_all | solution.py:46
  52.8 481.5 %all-reduce.5.cloned.1.call-start = ((), (), s32[]{:S(2)}) async-start(), calls=%async_computation.2 | async-start | bytes 2097152 | tf_op jit(solution)/shard_map/psum | solution.py:32
  57.0 570.3 %all-reduce.7.cloned.1.call-start = ((), (), s32[]{:S(2)}) async-start(), calls=%async_computation.3 | async-start | bytes 6553600
Sparse Core Ops, SparseCore 0:
  59.7 474.5 all-reduce.4
  536.6 90.5 all-reduce.6
where the time goes:
time: 637 us
  waiting for transfers between devices  453 us (71%)
  blocking collectives  114 us (18%)
  starting transfers between devices  26.5 us (4%)
  local copies, waits for them, and re-layouts  14.9 us (2%)
  between operations  14.9 us (2%)
  other arithmetic  7.51 us (1%)
  matrix products  6.53 us (1%)
    psum x1, waiting for transfers between devices, on_device(): total_sums, total_mass = lax.psum((coarse_sums, coarse_mass), ('dp', 'grp'))  312 us
    psum x1, blocking collectives, on_device(): total_sums, total_mass = lax.psum((coarse_sums, coarse_mass), ('dp', 'grp'))  105 us
    unnamed x3, waiting for transfers between devices  82.2 us
    all_to_all x1, waiting for transfers between devices, on_device(): lax.all_to_all(outgoing, 'dp', split_axis=0, concat_axis=1, tiled=True)  47.6 us
    all_to_all x1, starting transfers between devices, on_device(): lax.all_to_all(present_out, 'dp', split_axis=0, concat_axis=1, tiled=True)  20.6 us
  transfers between devices with their start and end apart: 4, of which 4 were waited for; matrix products, arithmetic and copies ran while one was open for 3% of the time, Pallas kernels for 0%

commit v1 on v0

v1 whole, which is shorter than its diff:
```python
import functools

import jax
import jax.numpy as jnp
from jax import lax
from jax.experimental import pallas as pl
from jax.experimental.pallas import tpu as pltpu
from jax.sharding import PartitionSpec as P

MESH = pl.DeviceIdType.MESH
prior_weight = 1.0
NZ, NP, NX = 16, 8, 4
MARK = 2.0**100
DISTANCE = [[7, 9, 8, 0], [5, 11, 6, 10], [3, 13, 4, 12], [1, 15, 2, 14]]
FLAT = [d for part in DISTANCE for d in part]


def iota(shape, dim):
    return lax.broadcasted_iota(jnp.int32, shape, dim)


def dot(a, b):
    return jnp.dot(a, b, preferred_element_type=jnp.float32)


def dot_t(a, b):
    return lax.dot_general(a, b, (((1,), (1,)), ((), ())), preferred_element_type=jnp.float32)


def column_softmax(scores):
    raised = jnp.exp(scores - jnp.max(scores, axis=0, keepdims=True))
    return raised * (1.0 / jnp.sum(raised, axis=0, keepdims=True))


def kernel(
    ids_ref, slot_ref, emb_ref, cc_ref, cent_hbm,
    coarse_out, child_out,
    cent, norms, acc, mass, out_a, in_a, zs, rows,
    csend, crecv, xsend, xrecv, zbuf, zrecv,
    cent_sem, a_send, a_recv, z_send, z_recv, x_send, x_recv, r_send, r_recv,
    c_send, c_recv, cx_send, cx_recv, cz_send, cz_recv, gx_send, gx_recv, gp_send, gp_recv,
):
    dp = lax.axis_index("dp")
    x = lax.axis_index("grp")
    z, p = dp // NP, dp % NP
    count, width = emb_ref.shape
    nchild = cent_hbm.shape[1]
    share = child_out.shape[1]
    scale = width ** (-0.5)

    def at_p(k):
        return (z * NP + (p + k) % NP, x)

    def at_z(d):
        return (((z + d) % NZ) * NP + p, x)

    def at_x(k):
        return (dp, (x + k) % NX)

    barrier = pltpu.get_barrier_semaphore()
    for k in range(1, NP):
        pl.semaphore_signal(barrier, inc=1, device_id=at_p(k), device_id_type=MESH)
    for k in range(1, NX):
        pl.semaphore_signal(barrier, inc=1, device_id=at_x(k), device_id_type=MESH)
    for k in range(1, NZ):
        pl.semaphore_signal(barrier, inc=1, device_id=at_z(k), device_id_type=MESH)
    cent_copy = pltpu.make_async_copy(cent_hbm, cent.at[:, pl.ds(0, nchild)], cent_sem)
    cent_copy.start()

    pending = []

    def send(src, dst, send_sem, recv_sem, device):
        copy = pltpu.make_async_remote_copy(
            src_ref=src, dst_ref=dst, send_sem=send_sem, recv_sem=recv_sem,
            device_id=device, device_id_type=MESH,
        )
        copy.start()
        pending.append(copy)

    def arrived(dst, sem):
        pltpu.make_async_remote_copy(
            src_ref=dst, dst_ref=dst, send_sem=sem, recv_sem=sem,
            device_id=at_x(1), device_id_type=MESH,
        ).wait_recv()

    square = (count, count)
    diagonal = iota(square, 0) == iota(square, 1)
    ids_row = ids_ref[...]
    ids_col = jnp.sum(jnp.where(diagonal, ids_row, 0), axis=1, keepdims=True)
    slot_col = jnp.sum(jnp.where(diagonal, slot_ref[...], 0), axis=1, keepdims=True)
    placed = jnp.sum(jnp.where(ids_row == iota(square, 0), slot_col, 0), axis=0, keepdims=True)
    before = (ids_col == ids_row) & (iota(square, 0) < iota(square, 1))
    position = jnp.sum(before.astype(jnp.int32), axis=0, keepdims=True)
    target = placed * 2 + position

    emb = emb_ref[...]
    for j in range(4):
        r = iota((NP * 16, 1), 0)
        peer, q, low = r // 16, (r // 4) % 4, r % 4
        d0, d1, d2, d3 = DISTANCE[j]
        distance = jnp.where(q == 0, d0, jnp.where(q == 1, d1, jnp.where(q == 2, d2, d3)))
        key = ((z + distance) % NZ) * (NP * 4) + peer * 4 + low
        pick = (key == target).astype(jnp.float32)
        empty = jnp.sum(pick, axis=1, keepdims=True) < 0.5
        block = dot(pick.astype(jnp.bfloat16), emb)
        block = jnp.where(empty & (iota((1, width), 1) == 0), MARK, block)
        out_a[j] = block.astype(jnp.bfloat16).reshape(NP, 16, width)

    pl.semaphore_wait(barrier, NP - 1 + NX - 1 + NZ - 1)

    for j in range(4):
        for k in range(1, NP):
            send(out_a.at[j, (p + k) % NP], in_a.at[j, p], a_send.at[j, k], a_recv.at[j, k], at_p(k))
        in_a[j, p] = out_a[j, p]

    cc = cc_ref[...]
    cc32 = cc.astype(jnp.float32)
    coarse_norms = jnp.sum(cc32 * cc32, axis=1, keepdims=True)
    weights = column_softmax((dot_t(cc, emb) - 0.5 * coarse_norms) * scale).astype(jnp.bfloat16)
    csend[:, :, :width] = dot(weights, emb).reshape(NP, 32, width)
    coarse_mass = jnp.sum(weights.astype(jnp.float32), axis=1, keepdims=True)
    csend[:, :, width:] = jnp.broadcast_to(coarse_mass, (count, 128)).reshape(NP, 32, 128)
    for k in range(1, NP):
        send(csend.at[(p + k) % NP], crecv.at[k], c_send.at[k], c_recv.at[k], at_p(k))

    o, i = iota((128, 128), 0), iota((128, 128), 1)
    source = ((o // 2) % 8) * 16 + (o // 32) * 4 + ((o // 16) % 2) * 2 + o % 2
    reorder = (i == source).astype(jnp.bfloat16)
    for j in range(4):
        for k in range(1, NP):
            arrived(in_a.at[j, (p - k + NP) % NP], a_recv.at[j, k])
        blocks = dot(reorder, in_a[j].reshape(128, width)).astype(jnp.bfloat16)
        blocks = blocks.reshape(4, 2, 16, width)
        zs[pl.ds(4 * j, 4)] = blocks
        for q in range(4):
            d, n = DISTANCE[j][q], 4 * j + q
            if d == 0:
                rows[0, n] = blocks[q]
            else:
                send(zs.at[n], rows.at[0, n], z_send.at[n], z_recv.at[n], at_z(d))

    cent_copy.wait()
    first = (iota((16, width), 0) == 0) & (iota((16, width), 1) == 0)
    for b in range(2):
        c32 = cent[b, :nchild].astype(jnp.float32)
        norms[b] = jnp.sum(c32 * c32, axis=1, keepdims=True)
        cent[b, nchild:] = first.astype(jnp.bfloat16)
    acc[...] = jnp.zeros_like(acc)
    mass[...] = jnp.zeros_like(mass)
    mine = (iota((128, nchild), 1) == iota((128, nchild), 0) + x * share) & (iota((128, nchild), 0) < share)
    mine = mine.astype(jnp.bfloat16)

    def score(j):
        def one(b, carry):
            block = rows[:, pl.ds(4 * j, 4), b].reshape(256, width)
            products = dot_t(cent[b], block)
            weights = column_softmax((products[:nchild] - 0.5 * norms[b]) * scale)
            weights = jnp.where(products[nchild : nchild + 1] < 0.5 * MARK, weights, 0.0)
            own = dot(mine, weights.astype(jnp.bfloat16))
            mass[b] += jnp.sum(own, axis=1, keepdims=True)
            acc[b] += dot(own.astype(jnp.bfloat16), block)
            return carry

        lax.fori_loop(0, 2, one, 0)

    def pass_on(n):
        if FLAT[n] != 0:
            arrived(rows.at[0, n], z_recv.at[n])
        send(rows.at[0, n], rows.at[1, n], x_send.at[n, 0], x_recv.at[n, 0], at_x(1))
        send(rows.at[0, n], rows.at[3, n], x_send.at[n, 1], x_recv.at[n, 1], at_x(3))

    def relay(n):
        arrived(rows.at[1, n], x_recv.at[n, 0])
        send(rows.at[1, n, 0], rows.at[2, n, 0], r_send.at[n, 0], r_recv.at[n, 0], at_x(1))
        arrived(rows.at[3, n], x_recv.at[n, 1])
        send(rows.at[3, n, 1], rows.at[2, n, 1], r_send.at[n, 1], r_recv.at[n, 1], at_x(3))

    def landed(n):
        arrived(rows.at[2, n, 0], r_recv.at[n, 0])
        arrived(rows.at[2, n, 1], r_recv.at[n, 1])

    def coarse_step(s):
        if s == 0:
            total = csend[p]
            for k in range(1, NP):
                arrived(crecv.at[k], c_recv.at[k])
                total = total + crecv[k]
            xsend[...] = total.reshape(NX, 8, width + 128)
            for k in range(1, NX):
                send(xsend.at[(x + k) % NX], xrecv.at[k], cx_send.at[k], cx_recv.at[k], at_x(k))
        elif s == 1:
            total = xsend[x]
            for k in range(1, NX):
                arrived(xrecv.at[k], cx_recv.at[k])
                total = total + xrecv[k]
            zbuf[0] = total
        if 1 <= s <= 5:
            if s > 1:
                arrived(zrecv.at[s - 2], cz_recv.at[s - 2])
                zbuf[s - 1] = zbuf[s - 2] + zrecv[s - 2]
            if s < 5:
                d = 1 << (s - 1)
                partner = z + d * (1 - 2 * ((z // d) % 2))
                send(
                    zbuf.at[s - 1], zrecv.at[s - 1], cz_send.at[s - 1], cz_recv.at[s - 1],
                    (partner * NP + p, x),
                )
            else:
                own = (iota((8, count), 1) == p * 32 + x * 8 + iota((8, count), 0)).astype(jnp.bfloat16)
                centers = dot(own, cc_ref[...])
                coarse_out[p, x] = (zbuf[4, :, :width] + prior_weight * centers) / (
                    zbuf[4, :, width : width + 1] + prior_weight
                )
                for k in range(1, NX):
                    send(coarse_out.at[p, x], coarse_out.at[p, x], gx_send.at[k], gx_recv.at[k], at_x(k))
        if s == 6:
            for k in range(1, NX):
                arrived(coarse_out.at[p, (x - k + NX) % NX], gx_recv.at[k])
            for k in range(1, NP):
                send(coarse_out.at[p], coarse_out.at[p], gp_send.at[k], gp_recv.at[k], at_p(k))
        if s == 7:
            for k in range(1, NP):
                arrived(coarse_out.at[(p - k + NP) % NP], gp_recv.at[k])

    steps = {3: 0, 5: 1, 6: 2, 7: 3, 8: 4, 9: 5, 11: 6}
    for n in range(NZ + 2):
        if n < NZ:
            pass_on(n)
        if 1 <= n <= NZ:
            relay(n - 1)
        if n >= 2:
            landed(n - 2)
            if (n - 2) % 4 == 3:
                score((n - 2) // 4)
        if n in steps:
            coarse_step(steps[n])
    centers = [dot(mine, cent[b, :nchild]) for b in range(2)]
    for b in range(2):
        value = (acc[b] + prior_weight * centers[b]) / (mass[b] + prior_weight)
        child_out[b] = value[:share]
    coarse_step(7)
    for copy in pending:
        copy.wait_send()


def on_device(embeddings, coarse_ids, owner_slot, coarse_centroids, child_centroids):
    count, width = embeddings.shape
    _, nchild, _ = child_centroids.shape
    share = nchild // NX
    f32, bf16 = jnp.float32, jnp.bfloat16
    vmem = pl.BlockSpec(memory_space=pltpu.VMEM)
    dma = pltpu.SemaphoreType.DMA
    coarse, children = pl.pallas_call(
        kernel,
        out_shape=(
            jax.ShapeDtypeStruct((NP, NX, 8, width), f32),
            jax.ShapeDtypeStruct((2, share, width), f32),
        ),
        in_specs=[vmem, vmem, vmem, vmem, pl.BlockSpec(memory_space=pl.ANY)],
        out_specs=(vmem, vmem),
        scratch_shapes=[
            pltpu.VMEM((2, nchild + 16, width), bf16),
            pltpu.VMEM((2, nchild, 1), f32),
            pltpu.VMEM((2, 128, width), f32),
            pltpu.VMEM((2, 128, 1), f32),
            pltpu.VMEM((4, NP, 16, width), bf16),
            pltpu.VMEM((4, NP, 16, width), bf16),
            pltpu.VMEM((NZ, 2, 16, width), bf16),
            pltpu.VMEM((NX, NZ, 2, 16, width), bf16),
            pltpu.VMEM((NP, 32, width + 128), f32),
            pltpu.VMEM((NP, 32, width + 128), f32),
            pltpu.VMEM((NX, 8, width + 128), f32),
            pltpu.VMEM((NX, 8, width + 128), f32),
            pltpu.VMEM((5, 8, width + 128), f32),
            pltpu.VMEM((4, 8, width + 128), f32),
            dma,
            dma((4, NP)), dma((4, NP)),
            dma((NZ,)), dma((NZ,)),
            dma((NZ, 2)), dma((NZ, 2)),
            dma((NZ, 2)), dma((NZ, 2)),
            dma((NP,)), dma((NP,)),
            dma((NX,)), dma((NX,)),
            dma((4,)), dma((4,)),
            dma((NX,)), dma((NX,)),
            dma((NP,)), dma((NP,)),
        ],
        compiler_params=pltpu.CompilerParams(
            collective_id=0, has_side_effects=True, vmem_limit_bytes=48 * 1024 * 1024
        ),
    )(
        coarse_ids.reshape(1, count),
        owner_slot.reshape(1, -1),
        embeddings,
        coarse_centroids,
        child_centroids,
    )
    return coarse.reshape(coarse_centroids.shape), children


def solution(mesh):
    return jax.shard_map(
        on_device,
        mesh=mesh,
        in_specs=(P(("dp", "grp"), None), P(("dp", "grp"), None), P(), P(), P("dp", None, None)),
        out_specs=(P(), P("dp", "grp", None)),
        check_vma=False,
    )
```

time: 637 us -> 122 us (0.19)
  the two profiles are of different devices: /device:TPU:1 before, /device:TPU:2 now
where the time goes in v1:
time: 122 us
  Pallas kernels  114 us (93%)
  local copies, waits for them, and re-layouts  7.36 us (6%)
    pallas_call x1, Pallas kernels, on_device(): pl.pallas_call(kernel, out_shape=(jax.ShapeDtypeStruct((NP, NX, 8, width)...  114 us
    unnamed x12, local copies, waits for them, and re-layouts  7.36 us

profile of v1, /device:TPU:2, one launch (start us, length us, event | category | flops | bytes accessed | tf_op | source)
XLA Modules:
  0.0 122.0 jit_solution(2940279097945679942)
XLA Ops:
  0.6 0.0 copy-start
  0.6 1.4 %copy-done = bf16[2,400,1024]{2,1,0:T(8,128)(2,1)S(1)} copy-done((bf16[2,400,1024]{2,1,0:T(8,128)(2,1)S(1)}, bf16[2,400,1024]{2,1,0:T(8,128)(2,1)}, u32[]{:S(2)}) %copy-start) | copy-done | bytes 1638424
  2.1 0.0 copy-start.1
  2.1 1.0 copy-done.1
  3.1 0.0 copy-start.2
  3.1 1.0 copy-done.2
  4.1 0.0 copy-start.3
  4.1 0.7 copy-done.3
  4.8 0.0 copy-start.4
  4.8 0.7 copy-done.4
  5.5 114.0 %shard_map.68 = (f32[8,4,8,1024]{3,2,1,0:T(8,128)S(1)}, f32[2,100,1024]{2,1,0:T(8,128)S(1)}) custom-call(s32[1,256]{1,0:T(1,128)S(1)} %bitcast.4, s32[1,256]{1,0:T(1,128)S(1)} %bitcast.5, bf16[256,1024]{1,0:T(8,128)(2,1)S(1)} %copy-done.1, bf16[256,1024]{1,0:T(8,128)(2,1)S(1)} %copy-done.2, bf16[2,400,1024]{2,1,0:T(8,128)(2,1)S(1)} %copy-done), custom_call_target="tpu_custom_call" | custom-call | tf_op jit(solution)/shard_map/pallas_call | solution.py:253
  119.5 1.5 %copy.7 = f32[2,100,1024]{2,0,1:T(2,128)} copy(f32[2,100,1024]{2,1,0:T(8,128)S(1)} %get-tuple-element.7) | data formatting | bytes 1638400
  121.0 1.0 copy.9
Async XLA Ops:
  0.6 1.4 %copy-start = (bf16[2,400,1024]{2,1,0:T(8,128)(2,1)S(1)}, bf16[2,400,1024]{2,1,0:T(8,128)(2,1)}, u32[]{:S(2)}) copy-start(bf16[2,400,1024]{2,1,0:T(8,128)(2,1)} %cent_hbm.1) | copy-start | bytes 4915204
  2.1 1.0 copy-start.1
  3.1 1.0 copy-start.2
  4.1 0.7 copy-start.3
  4.8 0.7 copy-start.4

commit v2 on v1

v2 whole, which is shorter than its diff:
```python
import jax
import jax.numpy as jnp
from jax import lax
from jax.experimental import pallas as pl
from jax.experimental.pallas import tpu as pltpu
from jax.sharding import PartitionSpec as P

MESH = pl.DeviceIdType.MESH
prior_weight = 1.0
NZ, NY, NC, NX = 16, 4, 2, 4
NP = NY * NC
MARK = 2.0**100
DISTANCE = (0, 1, 15, 2, 14, 3, 13, 4, 12, 5, 11, 6, 10, 7, 9, 8)
AHEAD = (8, 9, 10, 11, 12, 13, 14, 15, 15, 15, 15, 15, 15, 15, 15, 15)


def iota(shape, dim):
    return lax.broadcasted_iota(jnp.int32, shape, dim)


def dot(a, b):
    return jnp.dot(a, b, preferred_element_type=jnp.float32)


def dot_t(a, b):
    return lax.dot_general(a, b, (((1,), (1,)), ((), ())), preferred_element_type=jnp.float32)


def column_softmax(scores):
    raised = jnp.exp(scores - jnp.max(scores, axis=0, keepdims=True))
    return raised * (1.0 / jnp.sum(raised, axis=0, keepdims=True))


def kernel(
    ids_hbm, slot_hbm, emb_hbm, cc_hbm, cent_hbm,
    coarse_out, child_out,
    ids_ref, slot_ref, emb_ref, cc_ref, cent, norms, acc, mass, out_a, in_a, zs, rows,
    cbuf, crecv, ybuf, yrecv, xbuf, xrecv, zbuf, zrecv, tiles, centers8,
    load_sem, a_send, a_recv, z_send, z_recv, x_send, x_recv, r_send, r_recv,
    c_send, c_recv, cy_send, cy_recv, cx_send, cx_recv, cz_send, cz_recv,
    gz_send, gz_recv, gx_send, gx_recv, gy_send, gy_recv, gc_send, gc_recv,
):
    dp = lax.axis_index("dp")
    x = lax.axis_index("grp")
    z, p = dp // NP, dp % NP
    y, c = p // NC, p % NC
    count, width = emb_hbm.shape
    nchild = cent_hbm.shape[1]
    share = child_out.shape[0]
    scale = width ** (-0.5)

    def at_p(k):
        return (z * NP + (p + k) % NP, x)

    def at_z(to):
        return (to * NP + p, x)

    def at_x(k):
        return (dp, (x + k) % NX)

    def at_y(k):
        return (z * NP + ((y + k) % NY) * NC + c, x)

    other_core = (z * NP + y * NC + 1 - c, x)

    def signal(sem, device):
        pl.semaphore_signal(sem, inc=1, device_id=device, device_id_type=MESH)

    barrier = pltpu.get_barrier_semaphore()
    for k in range(1, NP):
        signal(barrier, at_p(k))
    for k in range(1, NX):
        signal(barrier, at_x(k))
    for k in range(1, NZ):
        signal(barrier, at_z((z + k) % NZ))

    loads = [
        pltpu.make_async_copy(ids_hbm, ids_ref, load_sem.at[0]),
        pltpu.make_async_copy(slot_hbm, slot_ref, load_sem.at[1]),
        pltpu.make_async_copy(emb_hbm, emb_ref, load_sem.at[2]),
        pltpu.make_async_copy(cc_hbm, cc_ref, load_sem.at[3]),
        pltpu.make_async_copy(cent_hbm, cent.at[:, pl.ds(0, nchild)], load_sem.at[4]),
    ]
    for load in loads:
        load.start()

    pending = []

    def send(src, dst, send_sem, recv_sem, device):
        copy = pltpu.make_async_remote_copy(
            src_ref=src, dst_ref=dst, send_sem=send_sem, recv_sem=recv_sem,
            device_id=device, device_id_type=MESH,
        )
        copy.start()
        return copy

    def keep(*args):
        pending.append(send(*args))

    def arrived(dst, sem):
        pltpu.make_async_remote_copy(
            src_ref=dst, dst_ref=dst, send_sem=sem, recv_sem=sem,
            device_id=at_x(1), device_id_type=MESH,
        ).wait_recv()

    for load in loads[:3]:
        load.wait()
    square = (count, count)
    diagonal = iota(square, 0) == iota(square, 1)
    ids_row = ids_ref[...]
    ids_col = jnp.sum(jnp.where(diagonal, ids_row, 0), axis=1, keepdims=True)
    slot_col = jnp.sum(jnp.where(diagonal, slot_ref[...], 0), axis=1, keepdims=True)
    placed = jnp.sum(jnp.where(ids_row == iota(square, 0), slot_col, 0), axis=0, keepdims=True)
    before = (ids_col == ids_row) & (iota(square, 0) < iota(square, 1))
    position = jnp.sum(before.astype(jnp.int32), axis=0, keepdims=True)
    target = placed * 2 + position

    emb = emb_ref[...]
    for j in range(4):
        r = iota((NP * 16, 1), 0)
        q = (r // 4) % 4
        d0, d1, d2, d3 = DISTANCE[4 * j : 4 * j + 4]
        distance = jnp.where(q == 0, d0, jnp.where(q == 1, d1, jnp.where(q == 2, d2, d3)))
        key = ((z + distance) % NZ) * (NP * 4) + (r // 16) * 4 + r % 4
        pick = (key == target).astype(jnp.float32)
        empty = jnp.sum(pick, axis=1, keepdims=True) < 0.5
        block = dot(pick.astype(jnp.bfloat16), emb)
        block = jnp.where(empty & (iota((1, width), 1) == 0), MARK, block)
        out_a[j] = block.astype(jnp.bfloat16).reshape(NP, 16, width)

    pl.semaphore_wait(barrier, NP - 1 + NX - 1 + NZ - 1)

    def stage_a(j):
        for k in range(1, NP):
            keep(out_a.at[j, (p + k) % NP], in_a.at[j, p], a_send.at[j, k], a_recv.at[j, k], at_p(k))
        in_a[j, p] = out_a[j, p]

    stage_a(0)
    stage_a(1)

    loads[3].wait()
    cc = cc_ref[...]
    cc32 = cc.astype(jnp.float32)
    coarse_norms = jnp.sum(cc32 * cc32, axis=1, keepdims=True)
    weights = column_softmax((dot_t(cc, emb) - 0.5 * coarse_norms) * scale).astype(jnp.bfloat16)
    cbuf[:, :, :, :width] = dot(weights, emb).reshape(NC, NY, 32, width)
    coarse_mass = jnp.sum(weights.astype(jnp.float32), axis=1, keepdims=True)
    cbuf[:, :, :, width:] = jnp.broadcast_to(coarse_mass, (count, 128)).reshape(NC, NY, 32, 128)
    keep(cbuf.at[1 - c], crecv, c_send, c_recv, other_core)
    own8 = (iota((8, count), 1) == c * 128 + y * 32 + x * 8 + iota((8, count), 0)).astype(jnp.bfloat16)
    rows8 = dot(own8, cc)
    for t in range(8):
        centers8[t] = rows8[:, 128 * t : 128 * (t + 1)]

    o, i = iota((128, 128), 0), iota((128, 128), 1)
    source = ((o // 2) % 8) * 16 + (o // 32) * 4 + ((o // 16) % 2) * 2 + o % 2
    reorder = (i == source).astype(jnp.bfloat16)

    def blocks_of(j):
        for k in range(1, NP):
            arrived(in_a.at[j, (p - k + NP) % NP], a_recv.at[j, k])
        blocks = dot(reorder, in_a[j].reshape(128, width)).astype(jnp.bfloat16)
        blocks = blocks.reshape(4, 2, 16, width)
        if j == 0:
            rows[0, 0] = blocks[0]
        zs[pl.ds(4 * j, 4)] = blocks

    def stage_z(n):
        keep(zs.at[n], rows.at[0, n], z_send.at[n], z_recv.at[n], at_z((z + DISTANCE[n]) % NZ))

    blocks_of(0)
    stage_a(2)

    def start_z(n):
        if n < NZ:
            if n % 4 == 0:
                blocks_of(n // 4)
                if n == 4:
                    stage_a(3)
            stage_z(n)

    for n in range(1, AHEAD[0] + 1):
        start_z(n)

    def coarse_step(s):
        if s == 0:
            arrived(crecv, c_recv)
            ybuf[...] = cbuf[c] + crecv[...]
            for k in range(1, NY):
                keep(ybuf.at[(y + k) % NY], yrecv.at[k], cy_send.at[k], cy_recv.at[k], at_y(k))
        if s == 1:
            total = ybuf[y]
            for k in range(1, NY):
                arrived(yrecv.at[k], cy_recv.at[k])
                total = total + yrecv[k]
            xbuf[...] = total.reshape(NX, 8, width + 128)
            for k in range(1, NX):
                keep(xbuf.at[(x + k) % NX], xrecv.at[k], cx_send.at[k], cx_recv.at[k], at_x(k))
        if s == 2:
            total = xbuf[x]
            for k in range(1, NX):
                arrived(xrecv.at[k], cx_recv.at[k])
                total = total + xrecv[k]
            for t in range(8):
                zbuf[t, 0] = total[:, 128 * t : 128 * (t + 1)]
                zbuf[t, 1] = total[:, width:]

                @pl.when(z == 2 * t)
                def _():
                    zrecv[z] = zbuf[t]

                @pl.when(z != 2 * t)
                def _():
                    send(zbuf.at[t], zrecv.at[z], cz_send.at[t], cz_recv.at[z], at_z(2 * t))
        if s == 3:

            @pl.when(z % 2 == 0)
            def _():
                for k in range(1, NZ):
                    arrived(zrecv.at[(z + k) % NZ], cz_recv.at[(z + k) % NZ])
                total = jnp.sum(zrecv[...], axis=0)
                tiles[z // 2] = (total[0] + prior_weight * centers8[z // 2]) / (total[1] + prior_weight)
                for k in range(1, NZ):
                    send(
                        tiles.at[z // 2], tiles.at[z // 2], gz_send.at[k], gz_recv.at[z // 2],
                        at_z((z + k) % NZ),
                    )
        if s == 4:
            for t in range(8):

                @pl.when(z != 2 * t)
                def _():
                    arrived(tiles.at[t], gz_recv.at[t])

            for t in range(8):
                coarse_out[c, y, x, :, pl.ds(128 * t, 128)] = tiles[t]
            for k in range(1, NX):
                keep(coarse_out.at[c, y, x], coarse_out.at[c, y, x], gx_send.at[k], gx_recv.at[k], at_x(k))
        if s == 5:
            for k in range(1, NX):
                arrived(coarse_out.at[c, y, (x - k + NX) % NX], gx_recv.at[k])
            for k in range(1, NY):
                keep(coarse_out.at[c, y], coarse_out.at[c, y], gy_send.at[k], gy_recv.at[k], at_y(k))
        if s == 6:
            for k in range(1, NY):
                arrived(coarse_out.at[c, (y - k + NY) % NY], gy_recv.at[k])
            keep(coarse_out.at[c], coarse_out.at[c], gc_send, gc_recv, other_core)
        if s == 7:
            arrived(coarse_out.at[1 - c], gc_recv)

    loads[4].wait()
    first = (iota((16, width), 0) == 0) & (iota((16, width), 1) == 0)
    for b in range(2):
        c32 = cent[b, :nchild].astype(jnp.float32)
        norms[b] = jnp.sum(c32 * c32, axis=1, keepdims=True)
        cent[b, nchild:] = first.astype(jnp.bfloat16)
    acc[...] = jnp.zeros_like(acc)
    mass[...] = jnp.zeros_like(mass)
    mine = (iota((128, nchild), 1) == iota((128, nchild), 0) + x * share) & (iota((128, nchild), 0) < share)
    mine = mine.astype(jnp.bfloat16)

    def score(j):
        def one(b, carry):
            block = rows[:, pl.ds(4 * j, 4), b].reshape(256, width)
            products = dot_t(cent[b], block)
            weights = column_softmax((products[:nchild] - 0.5 * norms[b]) * scale)
            weights = jnp.where(products[nchild : nchild + 1] < 0.5 * MARK, weights, 0.0)
            own = dot(mine, weights.astype(jnp.bfloat16))
            mass[b] += jnp.sum(own, axis=1, keepdims=True)
            acc[b] += dot(own.astype(jnp.bfloat16), block)
            return carry

        lax.fori_loop(0, 2, one, 0)

    def pass_on(n):
        if n > 0:
            arrived(rows.at[0, n], z_recv.at[n])
            for m in range(AHEAD[n - 1] + 1, AHEAD[n] + 1):
                start_z(m)
        keep(rows.at[0, n], rows.at[1, n], x_send.at[n, 0], x_recv.at[n, 0], at_x(1))
        keep(rows.at[0, n], rows.at[3, n], x_send.at[n, 1], x_recv.at[n, 1], at_x(3))

    def relay(n):
        arrived(rows.at[1, n], x_recv.at[n, 0])
        keep(rows.at[1, n, 0], rows.at[2, n, 0], r_send.at[n, 0], r_recv.at[n, 0], at_x(1))
        arrived(rows.at[3, n], x_recv.at[n, 1])
        keep(rows.at[3, n, 1], rows.at[2, n, 1], r_send.at[n, 1], r_recv.at[n, 1], at_x(3))

    def landed(n):
        arrived(rows.at[2, n, 0], r_recv.at[n, 0])
        arrived(rows.at[2, n, 1], r_recv.at[n, 1])

    steps = {1: 0, 3: 1, 5: 2, 11: 3, 14: 4, 16: 5, 17: 6}
    for n in range(NZ + 3):
        if n in steps:
            coarse_step(steps[n])
        if n < NZ:
            pass_on(n)
        if 1 <= n <= NZ:
            relay(n - 1)
        if 2 <= n < NZ + 2:
            landed(n - 2)
            if (n - 2) % 4 == 3:
                score((n - 2) // 4)
    for b in range(2):
        value = (acc[b] + prior_weight * dot(mine, cent[b, :nchild])) / (mass[b] + prior_weight)
        child_out[:, b] = value[:share]
    coarse_step(7)
    for copy in pending:
        copy.wait_send()
    def sent(src, sem):
        pltpu.make_async_remote_copy(
            src_ref=src, dst_ref=src, send_sem=sem, recv_sem=sem,
            device_id=at_x(1), device_id_type=MESH,
        ).wait_send()

    for t in range(8):

        @pl.when(z != 2 * t)
        def _():
            sent(zbuf.at[t], cz_send.at[t])

    @pl.when(z % 2 == 0)
    def _():
        for k in range(1, NZ):
            sent(tiles.at[z // 2], gz_send.at[k])


def on_device(embeddings, coarse_ids, owner_slot, coarse_centroids, child_centroids):
    count, width = embeddings.shape
    _, nchild, _ = child_centroids.shape
    share = nchild // NX
    f32, bf16 = jnp.float32, jnp.bfloat16
    vmem = pl.BlockSpec(memory_space=pltpu.VMEM)
    hbm = pl.BlockSpec(memory_space=pl.ANY)
    dma = pltpu.SemaphoreType.DMA
    wide = width + 128
    coarse, children = pl.pallas_call(
        kernel,
        out_shape=(
            jax.ShapeDtypeStruct((NC, NY, NX, 8, width), f32),
            jax.ShapeDtypeStruct((share, 2, width), f32),
        ),
        in_specs=[hbm] * 5,
        out_specs=(vmem, vmem),
        scratch_shapes=[
            pltpu.VMEM((1, count), jnp.int32),
            pltpu.VMEM((1, owner_slot.shape[0]), jnp.int32),
            pltpu.VMEM((count, width), bf16),
            pltpu.VMEM(coarse_centroids.shape, bf16),
            pltpu.VMEM((2, nchild + 16, width), bf16),
            pltpu.VMEM((2, nchild, 1), f32),
            pltpu.VMEM((2, 128, width), f32),
            pltpu.VMEM((2, 128, 1), f32),
            pltpu.VMEM((4, NP, 16, width), bf16),
            pltpu.VMEM((4, NP, 16, width), bf16),
            pltpu.VMEM((NZ, 2, 16, width), bf16),
            pltpu.VMEM((NX, NZ, 2, 16, width), bf16),
            pltpu.VMEM((NC, NY, 32, wide), f32),
            pltpu.VMEM((NY, 32, wide), f32),
            pltpu.VMEM((NY, 32, wide), f32),
            pltpu.VMEM((NY, 32, wide), f32),
            pltpu.VMEM((NX, 8, wide), f32),
            pltpu.VMEM((NX, 8, wide), f32),
            pltpu.VMEM((8, 2, 8, 128), f32),
            pltpu.VMEM((NZ, 2, 8, 128), f32),
            pltpu.VMEM((8, 8, 128), f32),
            pltpu.VMEM((8, 8, 128), f32),
            dma((5,)),
            dma((4, NP)), dma((4, NP)),
            dma((NZ,)), dma((NZ,)),
            dma((NZ, 2)), dma((NZ, 2)),
            dma((NZ, 2)), dma((NZ, 2)),
            dma, dma,
            dma((NY,)), dma((NY,)),
            dma((NX,)), dma((NX,)),
            dma((8,)), dma((NZ,)),
            dma((NZ,)), dma((8,)),
            dma((NX,)), dma((NX,)),
            dma((NY,)), dma((NY,)),
            dma, dma,
        ],
        compiler_params=pltpu.CompilerParams(
            collective_id=0, has_side_effects=True, vmem_limit_bytes=60 * 1024 * 1024
        ),
    )(
        coarse_ids.reshape(1, count),
        owner_slot.reshape(1, -1),
        embeddings,
        coarse_centroids,
        child_centroids,
    )
    return coarse.reshape(coarse_centroids.shape), children.transpose(1, 0, 2)


def solution(mesh):
    return jax.shard_map(
        on_device,
        mesh=mesh,
        in_specs=(P(("dp", "grp"), None), P(("dp", "grp"), None), P(), P(), P("dp", None, None)),
        out_specs=(P(), P("dp", "grp", None)),
        check_vma=False,
    )
```

time: 122 us -> 99.2 us (0.81)
  the two profiles are of different devices: /device:TPU:2 before, /device:TPU:1 now
where the time goes in v2:
time: 99.2 us; the launch traced here: 99 us
  Pallas kernels  95.1 us (96%)
  local copies, waits for them, and re-layouts  3.28 us (3%)
    pallas_call x1, Pallas kernels, on_device(): pl.pallas_call(kernel, out_shape=(jax.ShapeDtypeStruct((NC, NY, NX, 8, wi...  95.1 us
    unnamed x4, local copies, waits for them, and re-layouts  3.28 us

profile of v2, /device:TPU:1, one launch (start us, length us, event | category | flops | bytes accessed | tf_op | source)
XLA Modules:
  0.0 99.0 jit_solution(2592430804229155603)
XLA Ops:
  0.6 95.1 %shard_map.68 = (f32[2,4,4,8,1024]{4,3,2,1,0:T(8,128)}, f32[100,2,1024]{2,1,0:T(2,128)}) custom-call(s32[1,256]{1,0:T(1,128)} %bitcast.6, s32[1,256]{1,0:T(1,128)} %bitcast.7, bf16[256,1024]{1,0:T(8,128)(2,1)} %emb_hbm.1, bf16[256,1024]{1,0:T(8,128)(2,1)} %cc_hbm.1, bf16[2,400,1024]{2,1,0:T(8,128)(2,1)} %cent_hbm.1), custom_call_target="tpu_custom_call" | custom-call | tf_op jit(solution)/shard_map/pallas_call | solution.py:338
  95.7 0.0 copy-start
  95.7 2.4 %copy.9 = f32[256,1024]{1,0:T(8,128)} copy(f32[256,1024]{1,0:T(8,128)} %bitcast.4) | data formatting | bytes 2097152
  98.1 0.0 copy-done
  98.1 0.9 copy.10
Async XLA Ops:
  95.7 2.4 %copy-start = (f32[100,2,1024]{2,1,0:T(2,128)S(1)}, f32[100,2,1024]{2,1,0:T(2,128)}, u32[]{:S(2)}) copy-start(f32[100,2,1024]{2,1,0:T(2,128)} %get-tuple-element.5) | copy-start | bytes 2457604

commit v3 on v2

--- a/solution.py
+++ b/solution.py
@@ -241,12 +241,18 @@
                 arrived(coarse_out.at[c, y, (x - k + NX) % NX], gx_recv.at[k])
             for k in range(1, NY):
                 keep(coarse_out.at[c, y], coarse_out.at[c, y], gy_send.at[k], gy_recv.at[k], at_y(k))
+            to_core(0)
         if s == 6:
             for k in range(1, NY):
                 arrived(coarse_out.at[c, (y - k + NY) % NY], gy_recv.at[k])
-            keep(coarse_out.at[c], coarse_out.at[c], gc_send, gc_recv, other_core)
+                to_core(k)
         if s == 7:
-            arrived(coarse_out.at[1 - c], gc_recv)
+            for k in range(NY):
+                arrived(coarse_out.at[1 - c, (y - k + NY) % NY], gc_recv.at[k])
+
+    def to_core(k):
+        part = coarse_out.at[c, (y - k + NY) % NY]
+        keep(part, part, gc_send.at[k], gc_recv.at[k], other_core)
 
     loads[4].wait()
     first = (iota((16, width), 0) == 0) & (iota((16, width), 1) == 0)
@@ -290,7 +296,7 @@
         arrived(rows.at[2, n, 0], r_recv.at[n, 0])
         arrived(rows.at[2, n, 1], r_recv.at[n, 1])
 
-    steps = {1: 0, 3: 1, 5: 2, 11: 3, 14: 4, 16: 5, 17: 6}
+    steps = {0: 0, 2: 1, 3: 2, 10: 3, 13: 4, 15: 5, 17: 6}
     for n in range(NZ + 3):
         if n in steps:
             coarse_step(steps[n])
@@ -338,8 +344,8 @@
     coarse, children = pl.pallas_call(
         kernel,
         out_shape=(
-            jax.ShapeDtypeStruct((NC, NY, NX, 8, width), f32),
-            jax.ShapeDtypeStruct((share, 2, width), f32),
+            pltpu.VMEM((NC, NY, NX, 8, width), f32),
+            pltpu.VMEM((share, 2, width), f32),
         ),
         in_specs=[hbm] * 5,
         out_specs=(vmem, vmem),
@@ -378,7 +384,7 @@
             dma((NZ,)), dma((8,)),
             dma((NX,)), dma((NX,)),
             dma((NY,)), dma((NY,)),
-            dma, dma,
+            dma((NY,)), dma((NY,)),
         ],
         compiler_params=pltpu.CompilerParams(
             collective_id=0, has_side_effects=True, vmem_limit_bytes=60 * 1024 * 1024

time: 99.2 us -> 96.6 us (0.974)
  Pallas kernels: 95.1 us -> 93.2 us
  local copies, waits for them, and re-layouts: 3.28 us -> 1.86 us
    pallas_call x1, Pallas kernels: 95.1 us -> 93.2 us  [on_device(): pl.pallas_call(kernel, out_shape=(pltpu.VMEM((NC, NY, NX, 8, width), f32)...]
    unnamed x4 -> x2, local copies, waits for them, and re-layouts: 3.28 us -> 1.86 us
where the time goes in v3:
time: 96.6 us; the launch traced here: 95.7 us
  Pallas kernels  93.2 us (96%)
  local copies, waits for them, and re-layouts  1.86 us (2%)
    pallas_call x1, Pallas kernels, on_device(): pl.pallas_call(kernel, out_shape=(pltpu.VMEM((NC, NY, NX, 8, width), f32)...  93.2 us

profile of v3, /device:TPU:1, one launch (start us, length us, event | category | flops | bytes accessed | tf_op | source)
XLA Modules:
  0.0 95.7 jit_solution(12055553505749124784)
XLA Ops:
  0.6 93.2 %shard_map.68 = (f32[2,4,4,8,1024]{4,3,2,1,0:T(8,128)S(1)}, f32[100,2,1024]{2,1,0:T(2,128)S(1)}) custom-call(s32[1,256]{1,0:T(1,128)} %bitcast.6, s32[1,256]{1,0:T(1,128)} %bitcast.7, bf16[256,1024]{1,0:T(8,128)(2,1)} %emb_hbm.1, bf16[256,1024]{1,0:T(8,128)(2,1)} %cc_hbm.1, bf16[2,400,1024]{2,1,0:T(8,128)(2,1)} %cent_hbm.1), custom_call_target="tpu_custom_call" | custom-call | tf_op jit(solution)/shard_map/pallas_call | solution.py:344
  93.8 1.0 %copy.9 = f32[256,1024]{1,0:T(8,128)} copy(f32[256,1024]{1,0:T(8,128)S(1)} %bitcast.4) | data formatting | bytes 2097152
  94.8 0.9 copy.10

commit v4 on v3

--- a/solution.py
+++ b/solution.py
@@ -84,7 +84,7 @@
     for load in loads:
         load.start()
 
-    pending = []
+    pending, along_z = [], []
 
     def send(src, dst, send_sem, recv_sem, device):
         copy = pltpu.make_async_remote_copy(
@@ -166,7 +166,8 @@
         zs[pl.ds(4 * j, 4)] = blocks
 
     def stage_z(n):
-        keep(zs.at[n], rows.at[0, n], z_send.at[n], z_recv.at[n], at_z((z + DISTANCE[n]) % NZ))
+        copy = send(zs.at[n], rows.at[0, n], z_send.at[n], z_recv.at[n], at_z((z + DISTANCE[n]) % NZ))
+        along_z.append(copy)
 
     blocks_of(0)
     stage_a(2)
@@ -297,6 +298,7 @@
         arrived(rows.at[2, n, 1], r_recv.at[n, 1])
 
     steps = {0: 0, 2: 1, 3: 2, 10: 3, 13: 4, 15: 5, 17: 6}
+    started, done = [], 0
     for n in range(NZ + 3):
         if n in steps:
             coarse_step(steps[n])
@@ -308,11 +310,16 @@
             landed(n - 2)
             if (n - 2) % 4 == 3:
                 score((n - 2) // 4)
+        started.append(len(pending))
+        if n >= 4:
+            for copy in pending[done : started[n - 4]]:
+                copy.wait_send()
+            done = started[n - 4]
     for b in range(2):
         value = (acc[b] + prior_weight * dot(mine, cent[b, :nchild])) / (mass[b] + prior_weight)
         child_out[:, b] = value[:share]
     coarse_step(7)
-    for copy in pending:
+    for copy in pending[done:] + along_z:
         copy.wait_send()
     def sent(src, sem):
         pltpu.make_async_remote_copy(

time: 96.6 us -> 96.5 us (level)
  no operation moved by 1% of the time
where the time goes in v4:
time: 96.5 us; the launch traced here: 95.6 us
  Pallas kernels  93.1 us (96%)
  local copies, waits for them, and re-layouts  1.86 us (2%)
    pallas_call x1, Pallas kernels, on_device(): pl.pallas_call(kernel, out_shape=(pltpu.VMEM((NC, NY, NX, 8, width), f32)...  93.1 us

profile of v4, /device:TPU:1, one launch (start us, length us, event | category | flops | bytes accessed | tf_op | source)
XLA Modules:
  0.0 95.6 jit_solution(1414167172009533412)
XLA Ops:
  0.6 93.1 %shard_map.68 = (f32[2,4,4,8,1024]{4,3,2,1,0:T(8,128)S(1)}, f32[100,2,1024]{2,1,0:T(2,128)S(1)}) custom-call(s32[1,256]{1,0:T(1,128)} %bitcast.6, s32[1,256]{1,0:T(1,128)} %bitcast.7, bf16[256,1024]{1,0:T(8,128)(2,1)} %emb_hbm.1, bf16[256,1024]{1,0:T(8,128)(2,1)} %cc_hbm.1, bf16[2,400,1024]{2,1,0:T(8,128)(2,1)} %cent_hbm.1), custom_call_target="tpu_custom_call" | custom-call | tf_op jit(solution)/shard_map/pallas_call | solution.py:351
  93.7 1.0 %copy.9 = f32[256,1024]{1,0:T(8,128)} copy(f32[256,1024]{1,0:T(8,128)S(1)} %bitcast.4) | data formatting | bytes 2097152
  94.7 0.9 copy.10
